TPU v7x, 32 devices: a whole 2x2x4 slice. The times are simulated.
32 devices in a mesh: parts: 2 (over y), gx: 4 (over z), gy: 2 (over x), gz: 2 (over core).
Axes of the slice: x: 2, y: 2, z: 4, core: 2. Of those that a mesh axis runs over, the one named last changes fastest.
Arguments:
- e_adjoint: float32 [3, 64, 32, 256], P(None, ('parts', 'gx'), 'gz', 'gy'), parts along dimension 1, may hold values from -6 to 6
- h_adjoint: float32 [3, 64, 32, 256], P(None, ('parts', 'gx'), 'gz', 'gy'), parts along dimension 1, may hold values from -6 to 6
- forward_dft: bfloat16 [2, 16, 3, 64, 32, 256], P(None, None, None, ('parts', 'gx'), 'gz', 'gy'), parts along dimension 3, may hold values from -0.3984375 to 0.3984375
- material: int32 [64, 32, 256], P(('parts', 'gx'), 'gz', 'gy'), parts along dimension 0, may hold values from 0 to 3
- inv_permittivity: float32 [4], replicated, may hold values from 0.3 to 1
- conductivity: float32 [4], replicated, may hold values from 0.05 to 2
- omega: float32 [16], replicated, may hold values from 0.1 to 1.2
- freq_weight: float32 [16], replicated, may hold values from 0.3 to 1.5
- stencil: int32 [8, 64, 32, 256], P(None, ('parts', 'gx'), 'gz', 'gy'), parts along dimension 1, may hold values from 0 to 1023
- stencil_weight: bfloat16 [8, 64, 32, 256], P(None, ('parts', 'gx'), 'gz', 'gy'), parts along dimension 1, may hold values from 0.019897461 to 0.19921875
- owner_map: int32 [8, 2], P('parts'), parts along dimension 0, may hold values from 0 to 7
Outputs:
- e_final: float32 [3, 64, 32, 256], P(None, ('parts', 'gx'), 'gz', 'gy'), parts along dimension 1
- h_final: float32 [3, 64, 32, 256], P(None, ('parts', 'gx'), 'gz', 'gy'), parts along dimension 1
- material_grad: float32 [16, 1024], P(('parts', 'gx', 'gy'), 'gz'), parts along dimension 0
There are 2 independent parts, one for each index of `parts`. A program takes and returns all parts, laid end to end along the dimension named above; an argument that names none is the same for every part. Nothing has to cross between parts.
All inputs are finite; a program needn't handle non-finite values.
Results may differ from a plain program's by a relative error of at most 0.0021.
Values sent between devices are 32-bit elements; how exact they have to be, the bound alone decides.
A program may use at most 64 MiB of HBM per device.

v0:
```python
import jax
import jax.numpy as jnp
from jax import lax
from jax.sharding import PartitionSpec as P

PS = 1024
STEPS = 4


time_step = 0.55
low_width = 32


def shifted(x, axis, by):
    size = lax.axis_size(axis)
    pairs = [(i, i + by) for i in range(size) if 0 <= i + by < size]
    return lax.ppermute(x, axis, pairs)


def ahead_diff(field, upper, axis):
    size = field.shape[axis]
    following = jnp.concatenate([lax.slice_in_dim(field, 1, size, axis=axis), upper], axis=axis)
    return following - field


def behind_diff(field, lower, axis):
    size = field.shape[axis]
    previous = jnp.concatenate([lower, lax.slice_in_dim(field, 0, size - 1, axis=axis)], axis=axis)
    return field - previous


def curl_ahead(e_now):
    width_x, width_z, width_y = (e_now.shape[1], e_now.shape[2], e_now.shape[3])
    face_x = shifted(e_now[1:3, 0:1], "gx", -1)
    face_z = shifted(e_now[0:2, :, 0:1], "gz", -1)
    plane_y = jnp.stack([e_now[0, :, :, 0], e_now[2, :, :, 0]]).reshape(-1)
    face_y = shifted(plane_y, "gy", -1).reshape(2, width_x, width_z, 1)
    comp_x, comp_y, comp_z = (e_now[0], e_now[1], e_now[2])
    first = ahead_diff(comp_z, face_y[1], 2) - ahead_diff(comp_y, face_z[1], 1)
    second = ahead_diff(comp_x, face_z[0], 1) - ahead_diff(comp_z, face_x[1], 0)
    third = ahead_diff(comp_y, face_x[0], 0) - ahead_diff(comp_x, face_y[0], 2)
    return jnp.stack([first, second, third])


def curl_behind(h_now):
    width_x, width_z, width_y = (h_now.shape[1], h_now.shape[2], h_now.shape[3])
    face_x = shifted(h_now[1:3, width_x - 1 : width_x], "gx", 1)
    face_z = shifted(h_now[0:2, :, width_z - 1 : width_z], "gz", 1)
    plane_y = jnp.stack([h_now[0, :, :, width_y - 1], h_now[2, :, :, width_y - 1]]).reshape(-1)
    face_y = shifted(plane_y, "gy", 1).reshape(2, width_x, width_z, 1)
    comp_x, comp_y, comp_z = (h_now[0], h_now[1], h_now[2])
    first = behind_diff(comp_z, face_y[1], 2) - behind_diff(comp_y, face_z[1], 1)
    second = behind_diff(comp_x, face_z[0], 1) - behind_diff(comp_z, face_x[1], 0)
    third = behind_diff(comp_y, face_x[0], 0) - behind_diff(comp_x, face_y[0], 2)
    return jnp.stack([first, second, third])


def stencil_sums(stencil, stencil_weight, density):
    points = stencil.shape[0]
    high_width = PS // low_width
    index_rows = stencil.reshape(points, -1)
    weight_rows = stencil_weight.reshape(points, -1)
    values = density.reshape(-1)
    high_ids = jnp.arange(high_width, dtype=jnp.int32)
    low_ids = jnp.arange(low_width, dtype=jnp.int32)

    def add_point(total, item):
        index_now, weight_now = item
        scaled = weight_now.astype(jnp.float32) * values
        upper = (index_now[:, None] // low_width == high_ids[None, :]).astype(jnp.float32) * scaled[
            :, None
        ]
        lower = (index_now[:, None] % low_width == low_ids[None, :]).astype(jnp.float32)
        block = lax.dot_general(
            upper,
            lower,
            (((0,), (0,)), ((), ())),
            precision=lax.Precision.HIGHEST,
            preferred_element_type=jnp.float32,
        )
        return (total + block, None)

    summed, unused = lax.scan(
        add_point, jnp.zeros((high_width, low_width), jnp.float32), (index_rows, weight_rows)
    )
    return summed.reshape(PS)


def on_device(
    e_adjoint,
    h_adjoint,
    forward_dft,
    material,
    inv_permittivity,
    conductivity,
    omega,
    freq_weight,
    stencil,
    stencil_weight,
    owner_map,
):
    width_x, width_z, width_y = material.shape
    inv_cell = jnp.zeros(material.shape, jnp.float32)
    cond_cell = jnp.zeros(material.shape, jnp.float32)
    for which in range(inv_permittivity.shape[0]):
        chosen = material == which
        inv_cell = jnp.where(chosen, inv_permittivity[which], inv_cell)
        cond_cell = jnp.where(chosen, conductivity[which], cond_cell)
    loss = cond_cell * (time_step * 0.5) * inv_cell
    decay = (1.0 - loss) / (1.0 + loss)
    drive = time_step * inv_cell / (1.0 + loss)
    freqs = omega.shape[0]
    times = (jnp.arange(STEPS) + 1).astype(jnp.float32) * time_step
    angles = times[:, None] * omega[None, :]
    phase = jnp.concatenate(
        [freq_weight[None, :] * jnp.cos(angles), -freq_weight[None, :] * jnp.sin(angles)], axis=1
    ).astype(jnp.bfloat16)
    weighted = jnp.dot(
        phase, forward_dft.reshape(2 * freqs, -1), preferred_element_type=jnp.float32
    )
    weighted = weighted.reshape(STEPS, 3, width_x, width_z, width_y)
    e_now, h_now = (e_adjoint, h_adjoint)
    density = jnp.zeros(material.shape, jnp.float32)
    for step in range(STEPS):
        h_now = h_now - time_step * curl_ahead(e_now)
        e_now = decay * e_now + drive * curl_behind(h_now)
        density = density + (
            e_now[0] * weighted[step, 0]
            + e_now[1] * weighted[step, 1]
            + e_now[2] * weighted[step, 2]
        )
    partial_sums = stencil_sums(stencil, stencil_weight, density)
    depth = lax.axis_size("gz")
    half = PS // depth
    owner_flat = owner_map.reshape(-1)
    owners = owner_flat.shape[0]
    brick_index = lax.axis_index(("gx", "gy"))
    own = lax.dynamic_slice_in_dim(owner_flat, brick_index, 1)
    select = (jnp.arange(owners, dtype=jnp.int32) == own[0]).astype(jnp.float32)
    term = (select[:, None] * partial_sums[None, :]).reshape(owners * depth, half)
    grad = lax.psum_scatter(term, ("gx", "gy", "gz"), scatter_dimension=0, tiled=True)
    return (e_now, h_now, grad)


def solution(mesh):
    return jax.shard_map(
        on_device,
        mesh=mesh,
        in_specs=(
            P(None, ("parts", "gx"), "gz", "gy"),
            P(None, ("parts", "gx"), "gz", "gy"),
            P(None, None, None, ("parts", "gx"), "gz", "gy"),
            P(("parts", "gx"), "gz", "gy"),
            P(),
            P(),
            P(),
            P(),
            P(None, ("parts", "gx"), "gz", "gy"),
            P(None, ("parts", "gx"), "gz", "gy"),
            P("parts", None),
        ),
        out_specs=(
            P(None, ("parts", "gx"), "gz", "gy"),
            P(None, ("parts", "gx"), "gz", "gy"),
            P(("parts", "gx", "gy"), "gz"),
        ),
        check_vma=False,
    )
```

profile of v0, /device:TPU:0, one launch (start us, length us, event | category | flops | bytes accessed | tf_op | source)
XLA Modules:
  0.0 294.8 jit_solution(15111164460450836752)
XLA Ops:
  16.0 6.6 %multiply_divide_fusion = (f32[8,16,128]{2,1,0:T(8,128)}, pred[8,16,128]{2,1,0:T(8,128)(4,1)S(1)}, pred[8,16,128]{2,1,0:T(8,128)(4,1)S(1)}, pred[8,16,128]{2,1,0:T(8,128)(4,1)S(1)}, pred[8,16,128]{2,1,0:T(8,128)(4,1)S(1)}) fusion(f32[]{:T(128)} %bitcast.7, f32[]{:T(128)} %bitcast.6, f32[]{:T(128)} %bitcast.5, f32[]{:T(128)} %bitcast.4, f32[]{:T(128)} %bitcast.3, ...), kind=kLoop, calls=%fused_computation.154 | loop fusion | flops 278528 | bytes 196640 | tf_op jit(solution)/shard_map/div | solution.py:111
  22.6 5.1 %subtract_divide_fusion = f32[8,16,128]{2,1,0:T(8,128)S(1)} fusion(pred[8,16,128]{2,1,0:T(8,128)(4,1)S(1)} %get-tuple-element.181, pred[8,16,128]{2,1,0:T(8,128)(4,1)S(1)} %get-tuple-element.180, pred[8,16,128]{2,1,0:T(8,128)(4,1)S(1)} %get-tuple-element.179, pred[8,16,128]{2,1,0:T(8,128)(4,1)S(1)} %get-tuple-element.178, f32[]{:T(128)} %bitcast.7, ...), kind=kLoop, calls=%fused_computation.155 | loop fusion | flops 212992 | bytes 131104 | tf_op jit(solution)/shard_map/div | solution.py:110
  29.8 3.4 %reshape.557 = bf16[32,49152]{1,0:T(8,128)(2,1)S(1)} reshape(bf16[2,16,3,8,16,128]{5,4,3,2,1,0:T(8,128)(2,1)} %param.15) | data formatting | bytes 6291456 | tf_op jit(solution)/shard_map/reshape | solution.py:119
  34.1 1.8 fusion.14
  46.1 5.4 %collective-permute-start.3 = (f32[256]{0:T(256)S(1)}, f32[256]{0:T(256)S(1)}, u32[]{:S(2)}, u32[]{:S(2)}) collective-permute-start(f32[256]{0:T(256)S(1)} %reshape.547), channel_id=1, source_target_pairs={{0,2},{1,3},{4,6},{5,7},{8,10},{9,11},{12,14},{13,15},{16,18},{17,... | collective-permute-start | bytes 3080 | tf_op jit(solution)/shard_map/ppermute | solution.py:17
  51.5 3.3 %collective-permute-start.4 = (f32[2,8,1,128]{3,1,2,0:T(8,128)S(1)}, f32[2,8,1,128]{3,1,2,0:T(8,128)S(1)}, u32[]{:S(2)}, u32[]{:S(2)}) collective-permute-start(f32[2,8,1,128]{3,1,2,0:T(8,128)S(1)} %bitcast.267), channel_id=1, source_target_pairs={{0,1},{2,3},{4,5},{6,7},{8,9},{10,11},{12,13},{14,15},{16,17},{18,... | collective-permute-start | bytes 24584 | tf_op jit(solution)/shard_map/ppermute | solution.py:17
  54.8 5.0 %collective-permute-start.5 = (f32[2,1,16,128]{3,2,1,0:T(8,128)S(1)}, f32[2,1,16,128]{3,2,1,0:T(8,128)S(1)}, u32[]{:S(2)}, u32[]{:S(2)}) collective-permute-start(f32[2,1,16,128]{3,2,1,0:T(8,128)S(1)} %slice.904), channel_id=1, source_target_pairs={{0,4},{4,8},{8,12},{1,5},{5,9},{9,13},{2,6},{6,10},{10,14},{3,7},{... | collective-permute-start | bytes 49160 | tf_op jit(solution)/shard_map/ppermute | solution.py:17
  74.7 1.9 slice_bitcast_fusion.11
  84.1 3.4 %fusion.16 = (f32[1,8,16,128]{2,1,3,0:T(8,128)}, f32[1,8,16,128]{2,1,3,0:T(8,128)}, f32[1,8,16,128]{2,1,3,0:T(8,128)}) fusion(f32[1,8,16,1]{2,1,3,0:T(8,128)S(1)} %concatenate.317, f32[1,8,16,127]{2,1,3,0:T(8,128)} %slice_bitcast_fusion.11, f32[1,8,1,128]{2,1,3,0:T(8,128)S(1)} %copy.436, f32[1,8,15,128]{2,1,3,0:T(8,128)S(1)} %slice_bitcast_fusion.5, ...), kind=kLoop, calls=%fused_computation.34 | loop fusion | flops 245760 | bytes 786432 | tf_op jit(solution)/shard_map/sub | solution.py:39
  91.8 4.5 %collective-permute-start.9 = (f32[256]{0:T(256)S(1)}, f32[256]{0:T(256)S(1)}, u32[]{:S(2)}, u32[]{:S(2)}) collective-permute-start(f32[256]{0:T(256)S(1)} %reshape.549), channel_id=1, source_target_pairs={{0,2},{1,3},{4,6},{5,7},{8,10},{9,11},{12,14},{13,15},{16,18},{17,... | collective-permute-start | bytes 3080 | tf_op jit(solution)/shard_map/ppermute | solution.py:17
  96.3 3.3 %collective-permute-start.10 = (f32[2,8,1,128]{3,1,2,0:T(8,128)S(1)}, f32[2,8,1,128]{3,1,2,0:T(8,128)S(1)}, u32[]{:S(2)}, u32[]{:S(2)}) collective-permute-start(f32[2,8,1,128]{3,1,2,0:T(8,128)S(1)} %bitcast.268), channel_id=1, source_target_pairs={{0,1},{2,3},{4,5},{6,7},{8,9},{10,11},{12,13},{14,15},{16,17},{18,... | collective-permute-start | bytes 24584 | tf_op jit(solution)/shard_map/ppermute | solution.py:17
  99.6 5.0 %collective-permute-start.11 = (f32[2,1,16,128]{3,2,1,0:T(8,128)S(1)}, f32[2,1,16,128]{3,2,1,0:T(8,128)S(1)}, u32[]{:S(2)}, u32[]{:S(2)}) collective-permute-start(f32[2,1,16,128]{3,2,1,0:T(8,128)S(1)} %slice.938), channel_id=1, source_target_pairs={{0,4},{4,8},{8,12},{1,5},{5,9},{9,13},{2,6},{6,10},{10,14},{3,7},{... | collective-permute-start | bytes 49160 | tf_op jit(solution)/shard_map/ppermute | solution.py:17
  120.1 1.9 slice_bitcast_fusion.9
  129.5 3.5 %fusion.19 = (f32[1,8,16,128]{2,1,3,0:T(8,128)}, f32[1,8,16,128]{2,1,3,0:T(8,128)}, f32[1,8,16,128]{2,1,3,0:T(8,128)}) fusion(f32[1,8,16,1]{2,1,3,0:T(8,128)S(1)} %concatenate.341, f32[1,8,16,127]{2,1,3,0:T(8,128)} %slice_bitcast_fusion.9, f32[1,8,1,128]{2,1,3,0:T(8,128)S(1)} %copy.449, f32[1,8,15,128]{2,1,3,0:T(8,128)S(1)} %slice_bitcast_fusion.3, ...), kind=kLoop, calls=%fused_computation.43 | loop fusion | flops 245760 | bytes 786432 | tf_op jit(solution)/shard_map/sub | solution.py:39
  137.3 4.5 %collective-permute-start.15 = (f32[256]{0:T(256)S(1)}, f32[256]{0:T(256)S(1)}, u32[]{:S(2)}, u32[]{:S(2)}) collective-permute-start(f32[256]{0:T(256)S(1)} %reshape.551), channel_id=1, source_target_pairs={{0,2},{1,3},{4,6},{5,7},{8,10},{9,11},{12,14},{13,15},{16,18},{17,... | collective-permute-start | bytes 3080 | tf_op jit(solution)/shard_map/ppermute | solution.py:17
  141.8 3.3 %collective-permute-start.16 = (f32[2,8,1,128]{3,1,2,0:T(8,128)S(1)}, f32[2,8,1,128]{3,1,2,0:T(8,128)S(1)}, u32[]{:S(2)}, u32[]{:S(2)}) collective-permute-start(f32[2,8,1,128]{3,1,2,0:T(8,128)S(1)} %bitcast.269), channel_id=1, source_target_pairs={{0,1},{2,3},{4,5},{6,7},{8,9},{10,11},{12,13},{14,15},{16,17},{18,... | collective-permute-start | bytes 24584 | tf_op jit(solution)/shard_map/ppermute | solution.py:17
  145.1 4.8 %collective-permute-start.17 = (f32[2,1,16,128]{3,2,1,0:T(8,128)S(1)}, f32[2,1,16,128]{3,2,1,0:T(8,128)S(1)}, u32[]{:S(2)}, u32[]{:S(2)}) collective-permute-start(f32[2,1,16,128]{3,2,1,0:T(8,128)S(1)} %slice.972), channel_id=1, source_target_pairs={{0,4},{4,8},{8,12},{1,5},{5,9},{9,13},{2,6},{6,10},{10,14},{3,7},{... | collective-permute-start | bytes 49160 | tf_op jit(solution)/shard_map/ppermute | solution.py:17
  164.4 1.9 slice_bitcast_fusion.7
  173.1 3.4 %fusion.22 = (f32[1,8,16,128]{2,1,3,0:T(8,128)}, f32[1,8,16,128]{2,1,3,0:T(8,128)}, f32[1,8,16,128]{2,1,3,0:T(8,128)}) fusion(f32[1,8,16,1]{2,1,3,0:T(8,128)S(1)} %concatenate.365, f32[1,8,16,127]{2,1,3,0:T(8,128)} %slice_bitcast_fusion.7, f32[1,8,1,128]{2,1,3,0:T(8,128)S(1)} %copy.462, f32[1,8,15,128]{2,1,3,0:T(8,128)S(1)} %slice_bitcast_fusion.1, ...), kind=kLoop, calls=%fused_computation.52 | loop fusion | flops 245760 | bytes 786432 | tf_op jit(solution)/shard_map/sub | solution.py:39
  180.9 4.5 %collective-permute-start.21 = (f32[256]{0:T(256)S(1)}, f32[256]{0:T(256)S(1)}, u32[]{:S(2)}, u32[]{:S(2)}) collective-permute-start(f32[256]{0:T(256)S(1)} %reshape.553), channel_id=1, source_target_pairs={{0,2},{1,3},{4,6},{5,7},{8,10},{9,11},{12,14},{13,15},{16,18},{17,... | collective-permute-start | bytes 3080 | tf_op jit(solution)/shard_map/ppermute | solution.py:17
  185.4 2.7 collective-permute-start.22
  188.2 5.0 %collective-permute-start.23 = (f32[2,1,16,128]{3,2,1,0:T(8,128)S(1)}, f32[2,1,16,128]{3,2,1,0:T(8,128)S(1)}, u32[]{:S(2)}, u32[]{:S(2)}) collective-permute-start(f32[2,1,16,128]{3,2,1,0:T(8,128)S(1)} %slice.1006), channel_id=1, source_target_pairs={{0,4},{4,8},{8,12},{1,5},{5,9},{9,13},{2,6},{6,10},{10,14},{3,7},{... | collective-permute-start | bytes 49160 | tf_op jit(solution)/shard_map/ppermute | solution.py:17
  200.7 32.0 %while.15 = (s32[]{:T(128)}, f32[32,32]{1,0:T(8,128)S(1)}, s32[8,16384]{1,0:T(8,128)}, bf16[8,16384]{1,0:T(8,128)(2,1)}, f32[16384]{0:T(1024)S(1)}, /*index=5*/s32[]{:T(128)}, s32[]{:T(128)}) while((s32[]{:T(128)}, f32[32,32]{1,0:T(8,128)S(1)}, s32[8,16384]{1,0:T(8,128)}, bf16[8,16384]{1,0:T(8,128)(2,1)}, ...), condition=%wide.region_1.2_spmd.clone.clone, body=%wide.region_0.1_spmd.clone.clone.sunk | while | flops 203245568 | bytes 1876071 | solution.py:83
  232.9 60.7 %all-reduce = f32[16,512]{1,0:T(8,128)S(1)} all-reduce(f32[16,512]{1,0:T(8,128)S(1)} %broadcast_multiply_fusion.1), channel_id=2, replica_groups=mesh['parts'=2,'gx'=4,'gy'=2,'gz'=2] {'gx','gy','gz'}, use_global_device_ids=true, to_apply=%region_2.3.clone | all-reduce | flops 8192 | bytes 65536
  (424 shorter events, 146.9 us)
Async XLA Ops:
  2.1 42.6 %collective-permute-start.1 = (f32[2,8,1,128]{3,1,2,0:T(8,128)}, f32[2,8,1,128]{3,1,2,0:T(8,128)}, u32[]{:S(2)}, u32[]{:S(2)}) collective-permute-start(f32[2,8,1,128]{3,1,2,0:T(8,128)} %bitcast.118), channel_id=1, source_target_pairs={{1,0},{3,2},{5,4},{7,6},{9,8},{11,10},{13,12},{15,14},{17,16},{19,... | collective-permute-start | bytes 24584 | tf_op jit(solution)/shard_map/ppermute | solution.py:17
  4.8 40.7 %collective-permute-start.2 = (f32[2,1,16,128]{3,2,1,0:T(8,128)}, f32[2,1,16,128]{3,2,1,0:T(8,128)S(1)}, u32[]{:S(2)}, u32[]{:S(2)}) collective-permute-start(f32[2,1,16,128]{3,2,1,0:T(8,128)} %slice.731), channel_id=1, source_target_pairs={{4,0},{8,4},{12,8},{5,1},{9,5},{13,9},{6,2},{10,6},{14,10},{7,3},{... | collective-permute-start | bytes 49160 | tf_op jit(solution)/shard_map/ppermute | solution.py:17
  7.8 35.8 %collective-permute-start = (f32[256]{0:T(256)}, f32[256]{0:T(256)}, u32[]{:S(2)}, u32[]{:S(2)}) collective-permute-start(f32[256]{0:T(256)} %reshape.546), channel_id=1, source_target_pairs={{2,0},{3,1},{6,4},{7,5},{10,8},{11,9},{14,12},{15,13},{18,16},{19,... | collective-permute-start | bytes 3080 | tf_op jit(solution)/shard_map/ppermute | solution.py:17
  46.1 13.7 %collective-permute-start.3 = (f32[256]{0:T(256)S(1)}, f32[256]{0:T(256)S(1)}, u32[]{:S(2)}, u32[]{:S(2)}) collective-permute-start(f32[256]{0:T(256)S(1)} %reshape.547), channel_id=1, source_target_pairs={{0,2},{1,3},{4,6},{5,7},{8,10},{9,11},{12,14},{13,15},{16,18},{17,... | collective-permute-start | bytes 3080 | tf_op jit(solution)/shard_map/ppermute | solution.py:17
  51.5 8.8 %collective-permute-start.4 = (f32[2,8,1,128]{3,1,2,0:T(8,128)S(1)}, f32[2,8,1,128]{3,1,2,0:T(8,128)S(1)}, u32[]{:S(2)}, u32[]{:S(2)}) collective-permute-start(f32[2,8,1,128]{3,1,2,0:T(8,128)S(1)} %bitcast.267), channel_id=1, source_target_pairs={{0,1},{2,3},{4,5},{6,7},{8,9},{10,11},{12,13},{14,15},{16,17},{18,... | collective-permute-start | bytes 24584 | tf_op jit(solution)/shard_map/ppermute | solution.py:17
  54.8 6.4 %collective-permute-start.5 = (f32[2,1,16,128]{3,2,1,0:T(8,128)S(1)}, f32[2,1,16,128]{3,2,1,0:T(8,128)S(1)}, u32[]{:S(2)}, u32[]{:S(2)}) collective-permute-start(f32[2,1,16,128]{3,2,1,0:T(8,128)S(1)} %slice.904), channel_id=1, source_target_pairs={{0,4},{4,8},{8,12},{1,5},{5,9},{9,13},{2,6},{6,10},{10,14},{3,7},{... | collective-permute-start | bytes 49160 | tf_op jit(solution)/shard_map/ppermute | solution.py:17
  69.1 11.9 %collective-permute-start.6 = (f32[256]{0:T(256)}, f32[256]{0:T(256)S(1)}, u32[]{:S(2)}, u32[]{:S(2)}) collective-permute-start(f32[256]{0:T(256)} %reshape.548), channel_id=1, source_target_pairs={{2,0},{3,1},{6,4},{7,5},{10,8},{11,9},{14,12},{15,13},{18,16},{19,... | collective-permute-start | bytes 3080 | tf_op jit(solution)/shard_map/ppermute | solution.py:17
  70.4 12.8 %collective-permute-start.8 = (f32[2,1,16,128]{2,1,3,0:T(1,128)S(1)}, f32[2,1,16,128]{2,1,3,0:T(1,128)}, u32[]{:S(2)}, u32[]{:S(2)}) collective-permute-start(f32[2,1,16,128]{2,1,3,0:T(1,128)S(1)} %slice.922), channel_id=1, source_target_pairs={{4,0},{8,4},{12,8},{5,1},{9,5},{13,9},{6,2},{10,6},{14,10},{7,3},{... | collective-permute-start | bytes 49160 | tf_op jit(solution)/shard_map/ppermute | solution.py:17
  72.1 9.1 %collective-permute-start.7 = (f32[2,8,1,128]{3,1,2,0:T(8,128)S(1)}, f32[2,8,1,128]{3,1,2,0:T(8,128)}, u32[]{:S(2)}, u32[]{:S(2)}) collective-permute-start(f32[2,8,1,128]{3,1,2,0:T(8,128)S(1)} %copy.493), channel_id=1, source_target_pairs={{1,0},{3,2},{5,4},{7,6},{9,8},{11,10},{13,12},{15,14},{17,16},{19,... | collective-permute-start | bytes 24584 | tf_op jit(solution)/shard_map/ppermute | solution.py:17
  91.8 12.9 %collective-permute-start.9 = (f32[256]{0:T(256)S(1)}, f32[256]{0:T(256)S(1)}, u32[]{:S(2)}, u32[]{:S(2)}) collective-permute-start(f32[256]{0:T(256)S(1)} %reshape.549), channel_id=1, source_target_pairs={{0,2},{1,3},{4,6},{5,7},{8,10},{9,11},{12,14},{13,15},{16,18},{17,... | collective-permute-start | bytes 3080 | tf_op jit(solution)/shard_map/ppermute | solution.py:17
  96.3 8.8 %collective-permute-start.10 = (f32[2,8,1,128]{3,1,2,0:T(8,128)S(1)}, f32[2,8,1,128]{3,1,2,0:T(8,128)S(1)}, u32[]{:S(2)}, u32[]{:S(2)}) collective-permute-start(f32[2,8,1,128]{3,1,2,0:T(8,128)S(1)} %bitcast.268), channel_id=1, source_target_pairs={{0,1},{2,3},{4,5},{6,7},{8,9},{10,11},{12,13},{14,15},{16,17},{18,... | collective-permute-start | bytes 24584 | tf_op jit(solution)/shard_map/ppermute | solution.py:17
  99.6 6.3 %collective-permute-start.11 = (f32[2,1,16,128]{3,2,1,0:T(8,128)S(1)}, f32[2,1,16,128]{3,2,1,0:T(8,128)S(1)}, u32[]{:S(2)}, u32[]{:S(2)}) collective-permute-start(f32[2,1,16,128]{3,2,1,0:T(8,128)S(1)} %slice.938), channel_id=1, source_target_pairs={{0,4},{4,8},{8,12},{1,5},{5,9},{9,13},{2,6},{6,10},{10,14},{3,7},{... | collective-permute-start | bytes 49160 | tf_op jit(solution)/shard_map/ppermute | solution.py:17
  114.5 11.9 %collective-permute-start.12 = (f32[256]{0:T(256)}, f32[256]{0:T(256)S(1)}, u32[]{:S(2)}, u32[]{:S(2)}) collective-permute-start(f32[256]{0:T(256)} %reshape.550), channel_id=1, source_target_pairs={{2,0},{3,1},{6,4},{7,5},{10,8},{11,9},{14,12},{15,13},{18,16},{19,... | collective-permute-start | bytes 3080 | tf_op jit(solution)/shard_map/ppermute | solution.py:17
  115.8 12.8 %collective-permute-start.14 = (f32[2,1,16,128]{2,1,3,0:T(1,128)}, f32[2,1,16,128]{2,1,3,0:T(1,128)}, u32[]{:S(2)}, u32[]{:S(2)}) collective-permute-start(f32[2,1,16,128]{2,1,3,0:T(1,128)} %slice.956), channel_id=1, source_target_pairs={{4,0},{8,4},{12,8},{5,1},{9,5},{13,9},{6,2},{10,6},{14,10},{7,3},{... | collective-permute-start | bytes 49160 | tf_op jit(solution)/shard_map/ppermute | solution.py:17
  117.5 9.2 %collective-permute-start.13 = (f32[2,8,1,128]{3,1,2,0:T(8,128)S(1)}, f32[2,8,1,128]{3,1,2,0:T(8,128)}, u32[]{:S(2)}, u32[]{:S(2)}) collective-permute-start(f32[2,8,1,128]{3,1,2,0:T(8,128)S(1)} %copy.494), channel_id=1, source_target_pairs={{1,0},{3,2},{5,4},{7,6},{9,8},{11,10},{13,12},{15,14},{17,16},{19,... | collective-permute-start | bytes 24584 | tf_op jit(solution)/shard_map/ppermute | solution.py:17
  137.3 12.7 %collective-permute-start.15 = (f32[256]{0:T(256)S(1)}, f32[256]{0:T(256)S(1)}, u32[]{:S(2)}, u32[]{:S(2)}) collective-permute-start(f32[256]{0:T(256)S(1)} %reshape.551), channel_id=1, source_target_pairs={{0,2},{1,3},{4,6},{5,7},{8,10},{9,11},{12,14},{13,15},{16,18},{17,... | collective-permute-start | bytes 3080 | tf_op jit(solution)/shard_map/ppermute | solution.py:17
  141.8 8.6 %collective-permute-start.16 = (f32[2,8,1,128]{3,1,2,0:T(8,128)S(1)}, f32[2,8,1,128]{3,1,2,0:T(8,128)S(1)}, u32[]{:S(2)}, u32[]{:S(2)}) collective-permute-start(f32[2,8,1,128]{3,1,2,0:T(8,128)S(1)} %bitcast.269), channel_id=1, source_target_pairs={{0,1},{2,3},{4,5},{6,7},{8,9},{10,11},{12,13},{14,15},{16,17},{18,... | collective-permute-start | bytes 24584 | tf_op jit(solution)/shard_map/ppermute | solution.py:17
  145.1 6.3 %collective-permute-start.17 = (f32[2,1,16,128]{3,2,1,0:T(8,128)S(1)}, f32[2,1,16,128]{3,2,1,0:T(8,128)S(1)}, u32[]{:S(2)}, u32[]{:S(2)}) collective-permute-start(f32[2,1,16,128]{3,2,1,0:T(8,128)S(1)} %slice.972), channel_id=1, source_target_pairs={{0,4},{4,8},{8,12},{1,5},{5,9},{9,13},{2,6},{6,10},{10,14},{3,7},{... | collective-permute-start | bytes 49160 | tf_op jit(solution)/shard_map/ppermute | solution.py:17
  158.8 11.9 %collective-permute-start.18 = (f32[256]{0:T(256)S(1)}, f32[256]{0:T(256)S(1)}, u32[]{:S(2)}, u32[]{:S(2)}) collective-permute-start(f32[256]{0:T(256)S(1)} %reshape.552), channel_id=1, source_target_pairs={{2,0},{3,1},{6,4},{7,5},{10,8},{11,9},{14,12},{15,13},{18,16},{19,... | collective-permute-start | bytes 3080 | tf_op jit(solution)/shard_map/ppermute | solution.py:17
  160.1 12.1 %collective-permute-start.20 = (f32[2,1,16,128]{2,1,3,0:T(1,128)S(1)}, f32[2,1,16,128]{2,1,3,0:T(1,128)}, u32[]{:S(2)}, u32[]{:S(2)}) collective-permute-start(f32[2,1,16,128]{2,1,3,0:T(1,128)S(1)} %slice.990), channel_id=1, source_target_pairs={{4,0},{8,4},{12,8},{5,1},{9,5},{13,9},{6,2},{10,6},{14,10},{7,3},{... | collective-permute-start | bytes 49160 | tf_op jit(solution)/shard_map/ppermute | solution.py:17
  161.8 9.1 %collective-permute-start.19 = (f32[2,8,1,128]{3,1,2,0:T(8,128)S(1)}, f32[2,8,1,128]{3,1,2,0:T(8,128)S(1)}, u32[]{:S(2)}, u32[]{:S(2)}) collective-permute-start(f32[2,8,1,128]{3,1,2,0:T(8,128)S(1)} %copy.495), channel_id=1, source_target_pairs={{1,0},{3,2},{5,4},{7,6},{9,8},{11,10},{13,12},{15,14},{17,16},{19,... | collective-permute-start | bytes 24584 | tf_op jit(solution)/shard_map/ppermute | solution.py:17
  180.9 12.4 %collective-permute-start.21 = (f32[256]{0:T(256)S(1)}, f32[256]{0:T(256)S(1)}, u32[]{:S(2)}, u32[]{:S(2)}) collective-permute-start(f32[256]{0:T(256)S(1)} %reshape.553), channel_id=1, source_target_pairs={{0,2},{1,3},{4,6},{5,7},{8,10},{9,11},{12,14},{13,15},{16,18},{17,... | collective-permute-start | bytes 3080 | tf_op jit(solution)/shard_map/ppermute | solution.py:17
  185.4 8.3 %collective-permute-start.22 = (f32[2,8,1,128]{3,1,2,0:T(8,128)S(1)}, f32[2,8,1,128]{3,1,2,0:T(8,128)S(1)}, u32[]{:S(2)}, u32[]{:S(2)}) collective-permute-start(f32[2,8,1,128]{3,1,2,0:T(8,128)S(1)} %bitcast.270), channel_id=1, source_target_pairs={{0,1},{2,3},{4,5},{6,7},{8,9},{10,11},{12,13},{14,15},{16,17},{18,... | collective-permute-start | bytes 24584 | tf_op jit(solution)/shard_map/ppermute | solution.py:17
  188.2 6.3 %collective-permute-start.23 = (f32[2,1,16,128]{3,2,1,0:T(8,128)S(1)}, f32[2,1,16,128]{3,2,1,0:T(8,128)S(1)}, u32[]{:S(2)}, u32[]{:S(2)}) collective-permute-start(f32[2,1,16,128]{3,2,1,0:T(8,128)S(1)} %slice.1006), channel_id=1, source_target_pairs={{0,4},{4,8},{8,12},{1,5},{5,9},{9,13},{2,6},{6,10},{10,14},{3,7},{... | collective-permute-start | bytes 49160 | tf_op jit(solution)/shard_map/ppermute | solution.py:17
  (68 other events, 384.8 us)
where the time goes:
time: 298 us; the launch traced here: 295 us
  local copies, waits for them, and re-layouts  104 us (35%)
  starting transfers between devices  67.1 us (23%)
  blocking collectives  60.7 us (20%)
  other arithmetic  42.7 us (14%)
  matrix products  13.9 us (5%)
  waiting for transfers between devices  3.41 us (1%)
    ppermute x24, starting transfers between devices, shifted(): return lax.ppermute(x, axis, pairs)  67.1 us
    unnamed x1, blocking collectives  60.7 us
    slice x12, local copies, waits for them, and re-layouts, curl_ahead(): comp_x, comp_y, comp_z = (e_now[0], e_now[1], e_now[2])  18.2 us
    concatenate x22, local copies, waits for them, and re-layouts, ahead_diff(): jnp.concatenate([lax.slice_in_dim(field, 1, size, axis=axis), upper], axi...  14.9 us
    dot_general x8, matrix products, add_point(): lax.dot_general(upper, lower, (((0,), (0,)), ((), ())), precision=lax.Pre...  12 us
    sub x4, other arithmetic, curl_ahead(): first = ahead_diff(comp_z, face_y[1], 2) - ahead_diff(comp_y, face_z[1], 1)  10.4 us
    dynamic_slice x8, local copies, waits for them, and re-layouts, stencil_sums(): lax.scan(add_point, jnp.zeros((high_width, low_width), jnp.float32), (ind...  8.77 us
    unnamed x148, local copies, waits for them, and re-layouts  8.38 us
  transfers between devices with their start and end apart: 24, of which 4 were waited for; matrix products, arithmetic and copies ran while one was open for 24% of the time, Pallas kernels for 0%

commit v1 on v0

v1 whole, which is shorter than its diff:
```python
import functools

import jax
import jax.numpy as jnp
from jax import lax
from jax.experimental import pallas as pl
from jax.experimental.pallas import tpu as pltpu
from jax.sharding import PartitionSpec as P

PS = 1024
STEPS = 4
LOW = 32
time_step = 0.55
MESH = pl.DeviceIdType.MESH
F32 = jnp.float32
BF16 = jnp.bfloat16


def kernel(
    n_gx, n_gy, n_gz,
    phase, inv_eps, cond, owner_map,
    e_hbm, h_hbm, dft_hbm, mat_hbm, sten_hbm, w_hbm,
    e_ref, h_ref, grad_ref,
    dft, mat, sten, wgt, q_ref, decay_ref, drive_ref, g_ref,
    rows_ref, acc_ref, fold_ref,
    x_send, z_send, y_send, x_recv, z_recv, y_recv,
    p_send, p_recv,
    in_sems, send_sems, recv_sems, p_sems,
):
    freqs2, nc, nx, nz, ny = dft.shape
    points = sten.shape[0]
    part = lax.axis_index("parts")
    gx, gy, gz = lax.axis_index("gx"), lax.axis_index("gy"), lax.axis_index("gz")
    peers = n_gx * n_gy * n_gz
    me = (gx * n_gy + gy) * n_gz + gz

    def place(rank):
        return (part, rank // (n_gy * n_gz), (rank // n_gz) % n_gy, rank % n_gz)

    loads = [
        pltpu.make_async_copy(src, dst, in_sems.at[i])
        for i, (src, dst) in enumerate(
            [(e_hbm, e_ref), (h_hbm, h_ref), (mat_hbm, mat), (dft_hbm, dft), (sten_hbm, sten), (w_hbm, wgt)]
        )
    ]
    for load in loads:
        load.start()

    barrier = pltpu.get_barrier_semaphore()

    def greet(d, carry):
        pl.semaphore_signal(
            barrier, inc=1, device_id=place(lax.rem(me + d, peers)), device_id_type=MESH
        )
        return carry

    lax.fori_loop(1, peers, greet, 0)

    for has, slots, buf in (
        (gx < n_gx - 1, (0, 2, 4, 6), x_recv), (gx > 0, (1, 3, 5, 7), x_recv),
        (gz < n_gz - 1, (0, 2, 4, 6), z_recv), (gz > 0, (1, 3, 5, 7), z_recv),
        (gy < n_gy - 1, (0, 2, 4, 6), y_recv), (gy > 0, (1, 3, 5, 7), y_recv),
    ):
        @pl.when(jnp.logical_not(has))
        def _():
            for slot in slots:
                buf[slot] = jnp.zeros(buf.shape[1:], F32)

    pl.semaphore_wait(barrier, peers - 1)

    lane = lax.broadcasted_iota(jnp.int32, (nz, ny), 1)
    row = lax.broadcasted_iota(jnp.int32, (nz, ny), 0)

    def halo_copies(slot, ahead):
        by = -1 if ahead else 1

        def ends(at, size):
            low, high = at > 0, at < size - 1
            return (low, high) if ahead else (high, low)

        out = []
        for i, (snd, rcv, at, size, to) in enumerate((
            (x_send, x_recv, gx, n_gx, (part, gx + by, gy, gz)),
            (y_send, y_recv, gy, n_gy, (part, gx, gy + by, gz)),
            (z_send, z_recv, gz, n_gz, (part, gx, gy, gz + by)),
        )):
            copy = pltpu.make_async_remote_copy(
                src_ref=snd.at[slot], dst_ref=rcv.at[slot],
                send_sem=send_sems.at[slot, i], recv_sem=recv_sems.at[slot, i],
                device_id=to, device_id_type=MESH,
            )
            sends, receives = ends(at, size)
            out.append((copy, sends, receives))
        return out

    def start_halo(slot, ahead, ref):
        edge_x = 0 if ahead else nx - 1
        edge_z = 0 if ahead else nz - 1
        edge_y = 0 if ahead else ny - 1
        copies = halo_copies(slot, ahead)

        def go(which):
            copy, sends, _ = copies[which]

            @pl.when(sends)
            def _():
                copy.start()

        for c in range(2):
            x_send[slot, c] = ref[1 + c, edge_x]
        go(0)
        packed = jnp.zeros((nz, ny), F32)
        for c, comp in enumerate((0, 2)):
            for x in range(nx):
                at = c * nx + x
                moved = pltpu.roll(ref[comp, x], (at - edge_y) % ny, 1)
                packed = jnp.where(lane == at, moved, packed)
        y_send[slot] = packed
        go(1)
        for c in range(2):
            for x in range(nx):
                z_send[slot, pl.ds(c * nx + x, 1), :] = ref[c, x, pl.ds(edge_z, 1), :]
        go(2)

    def finish_halo(slot, ahead):
        for copy, _, receives in halo_copies(slot, ahead):
            @pl.when(receives)
            def _():
                copy.wait_recv()

    def curl(ref, slot, ahead, x, packed):
        def dx(comp):
            if ahead:
                nxt = ref[comp, x + 1] if x < nx - 1 else x_recv[slot, comp - 1]
                return nxt - ref[comp, x]
            prev = ref[comp, x - 1] if x > 0 else x_recv[slot, comp - 1]
            return ref[comp, x] - prev

        def dz(comp):
            halo = jnp.broadcast_to(z_recv[slot, pl.ds(comp * nx + x, 1), :], (nz, ny))
            here = ref[comp, x]
            if ahead:
                return jnp.where(row == nz - 1, halo, pltpu.roll(here, nz - 1, 0)) - here
            return here - jnp.where(row == 0, halo, pltpu.roll(here, 1, 0))

        def dy(comp):
            at = (comp // 2) * nx + x
            here = ref[comp, x]
            if ahead:
                halo = pltpu.roll(packed, (ny - 1 - at) % ny, 1)
                return jnp.where(lane == ny - 1, halo, pltpu.roll(here, ny - 1, 1)) - here
            halo = pltpu.roll(packed, (ny - at) % ny, 1)
            return here - jnp.where(lane == 0, halo, pltpu.roll(here, 1, 1))

        return dy(2) - dz(1), dz(0) - dx(2), dx(1) - dy(0)

    def weighted(c):
        def body(x, carry):
            sums = [jnp.zeros((nz, ny), F32) for _ in range(STEPS)]
            for f in range(freqs2):
                value = dft[f, c, x].astype(F32)
                for t in range(STEPS):
                    sums[t] = sums[t] + phase[t, f] * value
            for t in range(STEPS):
                q_ref[t, c, x] = sums[t]
            return carry

        lax.fori_loop(0, nx, body, 0)

    loads[0].wait()
    start_halo(0, True, e_ref)
    loads[1].wait()
    loads[2].wait()
    for x in range(nx):
        which = mat[x]
        inv_cell = jnp.zeros((nz, ny), F32)
        cond_cell = jnp.zeros((nz, ny), F32)
        for m in range(inv_eps.shape[0]):
            inv_cell = jnp.where(which == m, inv_eps[m], inv_cell)
            cond_cell = jnp.where(which == m, cond[m], cond_cell)
        loss = cond_cell * (time_step * 0.5) * inv_cell
        decay_ref[x] = (1.0 - loss) / (1.0 + loss)
        drive_ref[x] = time_step * inv_cell / (1.0 + loss)
        g_ref[x] = jnp.zeros((nz, ny), F32)
    loads[3].wait()
    weighted(0)
    for step in range(STEPS):
        finish_halo(2 * step, True)
        packed = y_recv[2 * step]
        for x in range(nx):
            parts = curl(e_ref, 2 * step, True, x, packed)
            for c in range(3):
                h_ref[c, x] = h_ref[c, x] - time_step * parts[c]
        start_halo(2 * step + 1, False, h_ref)
        if step == 0:
            weighted(1)
            weighted(2)
        finish_halo(2 * step + 1, False)
        packed = y_recv[2 * step + 1]
        for x in range(nx):
            parts = curl(h_ref, 2 * step + 1, False, x, packed)
            decay, drive = decay_ref[x], drive_ref[x]
            for c in range(3):
                e_ref[c, x] = decay * e_ref[c, x] + drive * parts[c]
        if step < STEPS - 1:
            start_halo(2 * step + 2, True, e_ref)
        for x in range(nx):
            g_ref[x] = g_ref[x] + (
                e_ref[0, x] * q_ref[step, 0, x]
                + e_ref[1, x] * q_ref[step, 1, x]
                + e_ref[2, x] * q_ref[step, 2, x]
            )

    loads[4].wait()
    loads[5].wait()
    high = PS // LOW
    ids = [
        (lax.broadcasted_iota(jnp.int32, (16, ny), 0) + 16 * i).astype(F32).astype(BF16)
        for i in range(2)
    ]
    zero = jnp.zeros((16, ny), BF16)
    one = jnp.ones((16, ny), BF16)
    groups = 4
    acc_ref[...] = jnp.zeros_like(acc_ref)

    def add_points(at, carry):
        k, x = at // nx, lax.rem(at, nx)
        index = sten[k, x]
        value = wgt[k, x].astype(F32) * g_ref[x]
        top = value.astype(BF16).astype(F32)
        rows_ref[0] = (index >> 5).astype(F32)
        rows_ref[1] = (index & (LOW - 1)).astype(F32)
        rows_ref[2] = top
        rows_ref[3] = value - top
        total = None
        for pair in range(nz // (2 * groups)):
            upper, rest, lower = [], [], []
            for half in range(2):
                ups, rests, lows = [], [], []
                for group in range(groups):
                    z = (group * (nz // (2 * groups)) + pair) * 2 + half
                    wide = [
                        jnp.broadcast_to(rows_ref[i, pl.ds(z, 1), :], (16, ny)).astype(BF16)
                        for i in range(4)
                    ]
                    for i in range(2):
                        hit = wide[0] == ids[i]
                        ups.append(jnp.where(hit, wide[2], zero))
                        rests.append(jnp.where(hit, wide[3], zero))
                        lows.append(jnp.where(wide[1] == ids[i], one, zero))
                upper.append(jnp.concatenate(ups, axis=0))
                rest.append(jnp.concatenate(rests, axis=0))
                lower.append(jnp.concatenate(lows, axis=0))
            left = jnp.concatenate(
                [jnp.concatenate(upper, axis=1), jnp.concatenate(rest, axis=1)], axis=0
            )
            right = jnp.concatenate(lower, axis=1)
            block = lax.dot_general(
                left, right, (((1,), (1,)), ((), ())), preferred_element_type=F32
            )
            total = block if total is None else total + block
        acc_ref[...] += total
        return carry

    lax.fori_loop(0, points * nx, add_points, 0)

    pieces = acc_ref[0 : groups * high, :] + acc_ref[groups * high :, :]
    width = groups * LOW
    lane_block = lax.broadcasted_iota(jnp.int32, (high, width), 1) // LOW
    row_block = lax.broadcasted_iota(jnp.int32, (high, width), 0) % groups
    summed = jnp.zeros((high, width), F32)
    for group in range(groups):
        summed = summed + jnp.where(
            lane_block == group, pieces[group * high : (group + 1) * high, :], 0.0
        )
    folded = summed
    for group in range(1, groups):
        folded = folded + pltpu.roll(summed, group * LOW, 1)
    folded = jnp.where(lane_block == row_block, folded, 0.0)
    fold_ref[...] = folded
    flat = fold_ref[pl.ds(0, high // groups, groups), :]
    for group in range(1, groups):
        flat = flat + fold_ref[pl.ds(group, high // groups, groups), :]
    tall = PS // n_gz // ny
    for i in range(n_gz):
        p_send[i] = flat[i * tall : (i + 1) * tall, :]

    def send_part(d, carry):
        to = lax.rem(me + d, peers)
        pltpu.make_async_remote_copy(
            src_ref=p_send.at[to % n_gz], dst_ref=p_recv.at[d - 1],
            send_sem=p_sems.at[0], recv_sem=p_sems.at[1],
            device_id=place(to), device_id_type=MESH,
        ).start()
        return carry

    lax.fori_loop(1, peers, send_part, 0)
    for slot in range(2 * STEPS):
        for copy, sends, _ in halo_copies(slot, slot % 2 == 0):
            @pl.when(sends)
            def _():
                copy.wait_send()
    pltpu.make_async_copy(p_recv, p_recv, p_sems.at[1]).wait()
    pltpu.make_async_copy(p_recv, p_recv, p_sems.at[0]).wait()

    my_owner = gx * n_gy + gy
    mine = jnp.where(owner_map[gx, gy] == my_owner, p_send[gz], 0.0)

    def add_part(d, total):
        brick = lax.rem(me - d + peers, peers) // n_gz
        owner = owner_map[brick // n_gy, brick % n_gy]
        return total + jnp.where(owner == my_owner, p_recv[d - 1], 0.0)

    mine = lax.fori_loop(1, peers, add_part, mine)
    for i in range(tall):
        grad_ref[:, i * ny : (i + 1) * ny] = mine[i : i + 1, :]


def on_device(
    e_adjoint, h_adjoint, forward_dft, material, inv_permittivity, conductivity,
    omega, freq_weight, stencil, stencil_weight, owner_map,
):
    nx, nz, ny = material.shape
    freqs = omega.shape[0]
    points = stencil.shape[0]
    n_gx, n_gy, n_gz = (lax.axis_size(a) for a in ("gx", "gy", "gz"))
    peers = n_gx * n_gy * n_gz
    times = (jnp.arange(STEPS) + 1).astype(F32) * time_step
    angles = times[:, None] * omega[None, :]
    phase = jnp.concatenate(
        [freq_weight[None, :] * jnp.cos(angles), -freq_weight[None, :] * jnp.sin(angles)], axis=1
    ).astype(BF16).astype(F32)
    dft = forward_dft.reshape(2 * freqs, 3, nx, nz, ny)
    smem = pl.BlockSpec(memory_space=pltpu.SMEM)
    hbm = pl.BlockSpec(memory_space=pl.ANY)
    vmem = pl.BlockSpec(memory_space=pltpu.VMEM)
    tall = PS // n_gz // ny
    slots = 2 * STEPS
    cell = (nx, nz, ny)
    return pl.pallas_call(
        functools.partial(kernel, n_gx, n_gy, n_gz),
        out_shape=(
            jax.ShapeDtypeStruct(e_adjoint.shape, F32),
            jax.ShapeDtypeStruct(h_adjoint.shape, F32),
            jax.ShapeDtypeStruct((1, PS // n_gz), F32),
        ),
        in_specs=[smem] * 4 + [hbm] * 6,
        out_specs=(vmem, vmem, vmem),
        scratch_shapes=[
            pltpu.VMEM(dft.shape, BF16),
            pltpu.VMEM(cell, jnp.int32),
            pltpu.VMEM(stencil.shape, jnp.int32),
            pltpu.VMEM(stencil_weight.shape, BF16),
            pltpu.VMEM((STEPS, 3) + cell, F32),
            pltpu.VMEM(cell, F32),
            pltpu.VMEM(cell, F32),
            pltpu.VMEM(cell, F32),
            pltpu.VMEM((4, nz, ny), F32),
            pltpu.VMEM((256, 128), F32),
            pltpu.VMEM((PS // LOW, 128), F32),
            pltpu.VMEM((slots, 2, nz, ny), F32),
            pltpu.VMEM((slots, 2 * nx, ny), F32),
            pltpu.VMEM((slots, nz, ny), F32),
            pltpu.VMEM((slots, 2, nz, ny), F32),
            pltpu.VMEM((slots, 2 * nx, ny), F32),
            pltpu.VMEM((slots, nz, ny), F32),
            pltpu.VMEM((n_gz, tall, ny), F32),
            pltpu.VMEM((peers - 1, tall, ny), F32),
            pltpu.SemaphoreType.DMA((6,)),
            pltpu.SemaphoreType.DMA((slots, 3)),
            pltpu.SemaphoreType.DMA((slots, 3)),
            pltpu.SemaphoreType.DMA((2,)),
        ],
        compiler_params=pltpu.CompilerParams(
            collective_id=0, has_side_effects=True, vmem_limit_bytes=32 * 1024 * 1024
        ),
    )(phase, inv_permittivity, conductivity, owner_map,
      e_adjoint, h_adjoint, dft, material, stencil, stencil_weight)


def solution(mesh):
    return jax.shard_map(
        on_device,
        mesh=mesh,
        in_specs=(
            P(None, ("parts", "gx"), "gz", "gy"),
            P(None, ("parts", "gx"), "gz", "gy"),
            P(None, None, None, ("parts", "gx"), "gz", "gy"),
            P(("parts", "gx"), "gz", "gy"),
            P(),
            P(),
            P(),
            P(),
            P(None, ("parts", "gx"), "gz", "gy"),
            P(None, ("parts", "gx"), "gz", "gy"),
            P("parts", None),
        ),
        out_specs=(
            P(None, ("parts", "gx"), "gz", "gy"),
            P(None, ("parts", "gx"), "gz", "gy"),
            P(("parts", "gx", "gy"), "gz"),
        ),
        check_vma=False,
    )
```

time: 298 us -> 63 us (0.21)
  local copies, waits for them, and re-layouts: 104 us -> 10.6 us
  starting transfers between devices: 67.1 us -> 0 us
  blocking collectives: 60.7 us -> 0 us
  Pallas kernels: 0 us -> 49.9 us
  other arithmetic: 42.7 us -> 1.52 us
  matrix products: 13.9 us -> 0 us
  waiting for transfers between devices: 3.41 us -> 0 us
    ppermute x24 -> x0, starting transfers between devices: 67.1 us -> none  [shifted(): return lax.ppermute(x, axis, pairs)]
    unnamed x1 -> x0, blocking collectives: 60.7 us -> none
    pallas_call x0 -> x1, Pallas kernels: none -> 49.9 us  [on_device(): pl.pallas_call(functools.partial(kernel, n_gx, n_gy, n_gz), out_shape=(ja...]
    slice x78 -> x0, local copies, waits for them, and re-layouts: 43.1 us -> none  [the longest x12 18.2 us: curl_ahead(): comp_x, comp_y, comp_z = (e_now[0], e_now[1], e_now[2])]
    concatenate x46 -> x0, local copies, waits for them, and re-layouts: 16.6 us -> none  [the longest x22 14.9 us: ahead_diff(): jnp.concatenate([lax.slice_in_dim(field, 1, size, axis=axis), upper], axi...]
    dot_general x9 -> x0, matrix products: 13.9 us -> none  [the longest x8 12 us: add_point(): lax.dot_general(upper, lower, (((0,), (0,)), ((), ())), precision=lax.Pre...]
    div x2 -> x0, other arithmetic: 11.7 us -> none  [the longest x1 6.6 us: on_device(): drive = time_step * inv_cell / (1.0 + loss)]
    sub x9 -> x0, local copies, waits for them, and re-layouts: 11.2 us -> none  [the longest x3 3.79 us: curl_ahead(): first = ahead_diff(comp_z, face_y[1], 2) - ahead_diff(comp_y, face_z[1], 1)]
  transfers between devices with their start and end apart: 24 -> 0, of which waited for: 4 -> 0; matrix products, arithmetic and copies ran while one was open for 24% -> 0% of each run, Pallas kernels for 0% -> 0%
where the time goes in v1:
time: 63 us; the launch traced here: 62.6 us
  Pallas kernels  49.9 us (79%)
  local copies, waits for them, and re-layouts  10.6 us (17%)
  other arithmetic  1.52 us (2%)
  between operations  0.65 us (1%)
    pallas_call x1, Pallas kernels, on_device(): pl.pallas_call(functools.partial(kernel, n_gx, n_gy, n_gz), out_shape=(ja...  49.9 us
    unnamed x20, local copies, waits for them, and re-layouts  10.6 us

profile of v1, /device:TPU:0, one launch (start us, length us, event | category | flops | bytes accessed | tf_op | source)
XLA Modules:
  0.0 62.6 jit_solution(1408704000413126996)
XLA Ops:
  0.6 0.7 %neg.4 = f32[16]{0:T(128)S(1)} negate(f32[16]{0:T(128)} %param.18) | non-fusion elementwise | flops 16 | bytes 128 | tf_op jit(solution)/shard_map/neg | solution.py:331
  1.3 0.8 %fusion.1 = (bf16[4,16]{1,0:T(4,128)(2,1)S(1)}, bf16[4,16]{1,0:T(4,128)(2,1)S(1)}) fusion(f32[16]{0:T(128)} %param.17, f32[4]{0:T(128)S(1)} %convert_multiply_fusion, f32[16]{0:T(128)} %param.18, f32[16]{0:T(128)S(1)} %neg.4), kind=kLoop, calls=%fused_computation.3 | loop fusion | flops 320 | bytes 464 | tf_op jit(solution)/shard_map/convert
  2.1 0.1 maximum_convert_fusion.phase
  2.2 0.8 %copy.14.owner_map = s32[4,2]{1,0:T(4,128)S(1)} copy(s32[4,2]{0,1:T(2,128)} %param.21) | data formatting | bytes 64 | tf_op args[10]
  2.9 0.0 copy-start
  2.9 1.9 %copy-done = bf16[2,16,3,8,16,128]{5,4,3,2,1,0:T(8,128)(2,1)S(1)} copy-done((bf16[2,16,3,8,16,128]{5,4,3,2,1,0:T(8,128)(2,1)S(1)}, bf16[2,16,3,8,16,128]{5,4,3,2,1,0:T(8,128)(2,1)}, u32[]{:S(2)}) %copy-start) | copy-done | bytes 3145752
  4.8 0.0 copy-start.1
  4.8 1.0 %copy-done.1 = s32[8,8,16,128]{3,2,1,0:T(8,128)S(1)} copy-done((s32[8,8,16,128]{3,2,1,0:T(8,128)S(1)}, s32[8,8,16,128]{3,2,1,0:T(8,128)}, u32[]{:S(2)}) %copy-start.1) | copy-done | bytes 524312
  5.9 0.0 copy-start.2
  5.9 0.9 %copy-done.2 = bf16[8,8,16,128]{3,2,1,0:T(8,128)(2,1)S(1)} copy-done((bf16[8,8,16,128]{3,2,1,0:T(8,128)(2,1)S(1)}, bf16[8,8,16,128]{3,2,1,0:T(8,128)(2,1)}, u32[]{:S(2)}) %copy-start.2) | copy-done | bytes 262168
  6.8 0.0 copy-start.3
  6.8 0.9 %copy-done.3 = f32[3,8,16,128]{3,2,1,0:T(8,128)S(1)} copy-done((f32[3,8,16,128]{3,2,1,0:T(8,128)S(1)}, f32[3,8,16,128]{3,2,1,0:T(8,128)}, u32[]{:S(2)}) %copy-start.3) | copy-done | bytes 196632
  7.7 0.0 copy-start.4
  7.7 0.9 %copy-done.4 = f32[3,8,16,128]{3,2,1,0:T(8,128)S(1)} copy-done((f32[3,8,16,128]{3,2,1,0:T(8,128)S(1)}, f32[3,8,16,128]{3,2,1,0:T(8,128)}, u32[]{:S(2)}) %copy-start.4) | copy-done | bytes 196632
  8.7 0.0 copy-start.5
  8.7 0.8 %copy-done.5 = s32[8,16,128]{2,1,0:T(8,128)S(1)} copy-done((s32[8,16,128]{2,1,0:T(8,128)S(1)}, s32[8,16,128]{2,1,0:T(8,128)}, u32[]{:S(2)}) %copy-start.5) | copy-done | bytes 65560
  9.5 0.0 copy-start.6
  9.5 0.7 %copy-done.6 = f32[4]{0:T(128)S(1)} copy-done((f32[4]{0:T(128)S(1)}, f32[4]{0:T(128)}, u32[]{:S(2)}) %copy-start.6) | copy-done | bytes 40
  10.2 0.0 copy-start.7
  10.2 0.7 %copy-done.7 = f32[4]{0:T(128)S(1)} copy-done((f32[4]{0:T(128)S(1)}, f32[4]{0:T(128)}, u32[]{:S(2)}) %copy-start.7) | copy-done | bytes 40
  10.8 49.9 %shard_map.130 = (f32[3,8,16,128]{3,2,1,0:T(8,128)S(1)}, f32[3,8,16,128]{3,2,1,0:T(8,128)S(1)}, f32[1,512]{1,0:T(1,128)S(1)}) custom-call(f32[4,32]{1,0:T(4,128)S(1)} %maximum_convert_fusion.phase, f32[4]{0:T(128)S(1)} %copy-done.6, f32[4]{0:T(128)S(1)} %copy-done.7, s32[4,2]{1,0:T(4,128)S(1)} %copy.14.owner_map, f32[3,8,16,128]{3,2,1,0:T(8,128)S(1)} %copy-done.3, ...), custom_call_target="tpu_custom_call" | custom-call | tf_op jit(solution)/shard_map/pallas_call | solution.py:340
  60.7 0.7 %copy.18 = f32[3,8,16,128]{3,2,1,0:T(8,128)} copy(f32[3,8,16,128]{3,2,1,0:T(8,128)S(1)} %get-tuple-element.8) | data formatting | bytes 393216
  61.4 0.7 %copy.19 = f32[3,8,16,128]{3,2,1,0:T(8,128)} copy(f32[3,8,16,128]{3,2,1,0:T(8,128)S(1)} %get-tuple-element.9) | data formatting | bytes 393216
  62.0 0.6 copy.20
  (1 shorter events, 0.0 us)
Async XLA Ops:
  2.9 1.9 %copy-start = (bf16[2,16,3,8,16,128]{5,4,3,2,1,0:T(8,128)(2,1)S(1)}, bf16[2,16,3,8,16,128]{5,4,3,2,1,0:T(8,128)(2,1)}, u32[]{:S(2)}) copy-start(bf16[2,16,3,8,16,128]{5,4,3,2,1,0:T(8,128)(2,1)} %param.13) | copy-start | bytes 9437188
  4.8 1.0 %copy-start.1 = (s32[8,8,16,128]{3,2,1,0:T(8,128)S(1)}, s32[8,8,16,128]{3,2,1,0:T(8,128)}, u32[]{:S(2)}) copy-start(s32[8,8,16,128]{3,2,1,0:T(8,128)} %sten_hbm.1) | copy-start | bytes 1572868
  5.9 0.9 %copy-start.2 = (bf16[8,8,16,128]{3,2,1,0:T(8,128)(2,1)S(1)}, bf16[8,8,16,128]{3,2,1,0:T(8,128)(2,1)}, u32[]{:S(2)}) copy-start(bf16[8,8,16,128]{3,2,1,0:T(8,128)(2,1)} %w_hbm.1) | copy-start | bytes 786436
  6.8 0.9 %copy-start.3 = (f32[3,8,16,128]{3,2,1,0:T(8,128)S(1)}, f32[3,8,16,128]{3,2,1,0:T(8,128)}, u32[]{:S(2)}) copy-start(f32[3,8,16,128]{3,2,1,0:T(8,128)} %e_hbm.1) | copy-start | bytes 589828
  7.7 0.9 %copy-start.4 = (f32[3,8,16,128]{3,2,1,0:T(8,128)S(1)}, f32[3,8,16,128]{3,2,1,0:T(8,128)}, u32[]{:S(2)}) copy-start(f32[3,8,16,128]{3,2,1,0:T(8,128)} %h_hbm.1) | copy-start | bytes 589828
  8.7 0.8 %copy-start.5 = (s32[8,16,128]{2,1,0:T(8,128)S(1)}, s32[8,16,128]{2,1,0:T(8,128)}, u32[]{:S(2)}) copy-start(s32[8,16,128]{2,1,0:T(8,128)} %mat_hbm.1) | copy-start | bytes 196612
  9.5 0.7 %copy-start.6 = (f32[4]{0:T(128)S(1)}, f32[4]{0:T(128)}, u32[]{:S(2)}) copy-start(f32[4]{0:T(128)} %inv_eps.1) | copy-start | bytes 52
  10.2 0.7 %copy-start.7 = (f32[4]{0:T(128)S(1)}, f32[4]{0:T(128)}, u32[]{:S(2)}) copy-start(f32[4]{0:T(128)} %cond.1) | copy-start | bytes 52

commit v2 on v1

--- a/solution.py
+++ b/solution.py
@@ -223,46 +223,47 @@
     groups = 4
     acc_ref[...] = jnp.zeros_like(acc_ref)
 
-    def add_points(at, carry):
-        k, x = at // nx, lax.rem(at, nx)
-        index = sten[k, x]
-        value = wgt[k, x].astype(F32) * g_ref[x]
-        top = value.astype(BF16).astype(F32)
-        rows_ref[0] = (index >> 5).astype(F32)
-        rows_ref[1] = (index & (LOW - 1)).astype(F32)
-        rows_ref[2] = top
-        rows_ref[3] = value - top
+    def add_points(x, carry):
         total = None
-        for pair in range(nz // (2 * groups)):
-            upper, rest, lower = [], [], []
-            for half in range(2):
-                ups, rests, lows = [], [], []
-                for group in range(groups):
-                    z = (group * (nz // (2 * groups)) + pair) * 2 + half
-                    wide = [
-                        jnp.broadcast_to(rows_ref[i, pl.ds(z, 1), :], (16, ny)).astype(BF16)
-                        for i in range(4)
-                    ]
-                    for i in range(2):
-                        hit = wide[0] == ids[i]
-                        ups.append(jnp.where(hit, wide[2], zero))
-                        rests.append(jnp.where(hit, wide[3], zero))
-                        lows.append(jnp.where(wide[1] == ids[i], one, zero))
-                upper.append(jnp.concatenate(ups, axis=0))
-                rest.append(jnp.concatenate(rests, axis=0))
-                lower.append(jnp.concatenate(lows, axis=0))
-            left = jnp.concatenate(
-                [jnp.concatenate(upper, axis=1), jnp.concatenate(rest, axis=1)], axis=0
-            )
-            right = jnp.concatenate(lower, axis=1)
-            block = lax.dot_general(
-                left, right, (((1,), (1,)), ((), ())), preferred_element_type=F32
-            )
-            total = block if total is None else total + block
+        for k in range(points):
+            index = sten[k, x]
+            value = wgt[k, x].astype(F32) * g_ref[x]
+            top = value.astype(BF16).astype(F32)
+            rows_ref[k, 0] = (index >> 5).astype(F32)
+            rows_ref[k, 1] = (index & (LOW - 1)).astype(F32)
+            rows_ref[k, 2] = top
+            rows_ref[k, 3] = value - top
+        for k in range(points):
+            for pair in range(nz // (2 * groups)):
+                upper, rest, lower = [], [], []
+                for half in range(2):
+                    ups, rests, lows = [], [], []
+                    for group in range(groups):
+                        z = (group * (nz // (2 * groups)) + pair) * 2 + half
+                        wide = [
+                            jnp.broadcast_to(rows_ref[k, i, pl.ds(z, 1), :], (16, ny)).astype(BF16)
+                            for i in range(4)
+                        ]
+                        for i in range(2):
+                            hit = wide[0] == ids[i]
+                            ups.append(jnp.where(hit, wide[2], zero))
+                            rests.append(jnp.where(hit, wide[3], zero))
+                            lows.append(jnp.where(wide[1] == ids[i], one, zero))
+                    upper.append(jnp.concatenate(ups, axis=0))
+                    rest.append(jnp.concatenate(rests, axis=0))
+                    lower.append(jnp.concatenate(lows, axis=0))
+                left = jnp.concatenate(
+                    [jnp.concatenate(upper, axis=1), jnp.concatenate(rest, axis=1)], axis=0
+                )
+                right = jnp.concatenate(lower, axis=1)
+                block = lax.dot_general(
+                    left, right, (((1,), (1,)), ((), ())), preferred_element_type=F32
+                )
+                total = block if total is None else total + block
         acc_ref[...] += total
         return carry
 
-    lax.fori_loop(0, points * nx, add_points, 0)
+    lax.fori_loop(0, nx, add_points, 0)
 
     pieces = acc_ref[0 : groups * high, :] + acc_ref[groups * high :, :]
     width = groups * LOW
@@ -355,7 +356,7 @@
             pltpu.VMEM(cell, F32),
             pltpu.VMEM(cell, F32),
             pltpu.VMEM(cell, F32),
-            pltpu.VMEM((4, nz, ny), F32),
+            pltpu.VMEM((points, 4, nz, ny), F32),
             pltpu.VMEM((256, 128), F32),
             pltpu.VMEM((PS // LOW, 128), F32),
             pltpu.VMEM((slots, 2, nz, ny), F32),
@@ -372,7 +373,7 @@
             pltpu.SemaphoreType.DMA((2,)),
         ],
         compiler_params=pltpu.CompilerParams(
-            collective_id=0, has_side_effects=True, vmem_limit_bytes=32 * 1024 * 1024
+            collective_id=0, has_side_effects=True, vmem_limit_bytes=60 * 1024 * 1024
         ),
     )(phase, inv_permittivity, conductivity, owner_map,
       e_adjoint, h_adjoint, dft, material, stencil, stencil_weight)

time: 63 us -> 48.9 us (0.78)
  Pallas kernels: 49.9 us -> 40.1 us
  local copies, waits for them, and re-layouts: 10.6 us -> 5.83 us
    pallas_call x1, Pallas kernels: 49.9 us -> 40.1 us  [on_device(): pl.pallas_call(functools.partial(kernel, n_gx, n_gy, n_gz), out_shape=(ja...]
    unnamed x20 -> x4, local copies, waits for them, and re-layouts: 10.6 us -> 5.83 us
where the time goes in v2:
time: 48.9 us; the launch traced here: 48.7 us
  Pallas kernels  40.1 us (82%)
  local copies, waits for them, and re-layouts  5.83 us (12%)
  other arithmetic  2.1 us (4%)
  between operations  0.64 us (1%)
    pallas_call x1, Pallas kernels, on_device(): pl.pallas_call(functools.partial(kernel, n_gx, n_gy, n_gz), out_shape=(ja...  40.1 us
    unnamed x4, local copies, waits for them, and re-layouts  5.83 us

profile of v2, /device:TPU:0, one launch (start us, length us, event | category | flops | bytes accessed | tf_op | source)
XLA Modules:
  0.0 48.7 jit_solution(1726146291539302217)
XLA Ops:
  0.6 0.7 %neg.4 = f32[16]{0:T(128)S(1)} negate(f32[16]{0:T(128)} %param.18) | non-fusion elementwise | flops 16 | bytes 128 | tf_op jit(solution)/shard_map/neg | solution.py:332
  1.3 0.8 %fusion.1 = (bf16[4,16]{1,0:T(4,128)(2,1)S(1)}, bf16[4,16]{1,0:T(4,128)(2,1)S(1)}) fusion(f32[16]{0:T(128)} %param.17, f32[4]{0:T(128)S(1)} %convert_multiply_fusion, f32[16]{0:T(128)} %param.18, f32[16]{0:T(128)S(1)} %neg.4), kind=kLoop, calls=%fused_computation.3 | loop fusion | flops 320 | bytes 464 | tf_op jit(solution)/shard_map/convert
  2.1 0.7 %maximum_convert_fusion.phase = f32[4,32]{1,0:T(4,128)} fusion(bf16[4,16]{1,0:T(4,128)(2,1)S(1)} %get-tuple-element.4, bf16[4,16]{1,0:T(4,128)(2,1)S(1)} %get-tuple-element.3), kind=kLoop, calls=%fused_computation.6 | loop fusion | flops 512 | bytes 768 | tf_op jit(solution)/shard_map/convert_element_type | solution.py:333
  2.7 1.3 %copy.14.owner_map = s32[4,2]{1,0:T(4,128)} copy(s32[4,2]{0,1:T(2,128)} %param.21) | data formatting | bytes 64 | tf_op args[10]
  4.1 40.1 %shard_map.130 = (f32[3,8,16,128]{3,2,1,0:T(8,128)}, f32[3,8,16,128]{3,2,1,0:T(8,128)}, f32[1,512]{1,0:T(1,128)}) custom-call(f32[4,32]{1,0:T(4,128)} %maximum_convert_fusion.phase, f32[4]{0:T(128)} %inv_eps.1, f32[4]{0:T(128)} %cond.1, s32[4,2]{1,0:T(4,128)} %copy.14.owner_map, f32[3,8,16,128]{3,2,1,0:T(8,128)} %e_hbm.1, f32[3,8,16,128]{3,2,1,0:T(8,128)} %h_hbm.1, ...), custom_call_target="tpu_custom_call" | custom-call | tf_op jit(solution)/shard_map/pallas_call | solution.py:341
  44.2 1.6 %copy.18 = f32[3,8,16,128]{3,2,1,0:T(8,128)} copy(f32[3,8,16,128]{3,2,1,0:T(8,128)} %get-tuple-element.8) | data formatting | bytes 393216
  45.8 1.6 %copy.19 = f32[3,8,16,128]{3,2,1,0:T(8,128)} copy(f32[3,8,16,128]{3,2,1,0:T(8,128)} %get-tuple-element.9) | data formatting | bytes 393216
  47.4 1.3 %copy.20 = f32[1,512]{1,0:T(1,128)} copy(f32[1,512]{1,0:T(1,128)} %get-tuple-element.10) | data formatting | bytes 4096
  (1 shorter events, 0.0 us)

commit v3 on v2

--- a/solution.py
+++ b/solution.py
@@ -24,8 +24,9 @@
     dft, mat, sten, wgt, q_ref, decay_ref, drive_ref, g_ref,
     rows_ref, acc_ref, fold_ref,
     x_send, z_send, y_send, x_recv, z_recv, y_recv,
+    row_send, col_send, row_recv, col_recv,
     p_send, p_recv,
-    in_sems, send_sems, recv_sems, p_sems,
+    in_sems, send_sems, recv_sems, edge_sems, p_sems,
 ):
     freqs2, nc, nx, nz, ny = dft.shape
     points = sten.shape[0]
@@ -65,6 +66,18 @@
         def _():
             for slot in slots:
                 buf[slot] = jnp.zeros(buf.shape[1:], F32)
+
+    low = (gx > 0, gy > 0, gz > 0)
+    high_side = (gx < n_gx - 1, gy < n_gy - 1, gz < n_gz - 1)
+    edges = (
+        (row_send, row_recv, 0, 0, 2), (row_send, row_recv, 1, 1, 2),
+        (col_send, col_recv, 0, 0, 1), (col_send, col_recv, 1, 1, 0),
+    )
+    for _, rcv, which, up, down in edges:
+        @pl.when(jnp.logical_not(low[up] & high_side[down]))
+        def _():
+            for step in range(STEPS):
+                rcv[step, which] = jnp.zeros(rcv.shape[2:], F32)
 
     pl.semaphore_wait(barrier, peers - 1)
 
@@ -93,40 +106,108 @@
             out.append((copy, sends, receives))
         return out
 
-    def start_halo(slot, ahead, ref):
-        edge_x = 0 if ahead else nx - 1
+    def edge_copies(step):
+        out = []
+        for i, (snd, rcv, which, up, down) in enumerate(edges):
+            to = [gx, gy, gz]
+            to[up] = to[up] + 1
+            to[down] = to[down] - 1
+            copy = pltpu.make_async_remote_copy(
+                src_ref=snd.at[step, which], dst_ref=rcv.at[step, which],
+                send_sem=edge_sems.at[0, step, i], recv_sem=edge_sems.at[1, step, i],
+                device_id=(part, *to), device_id_type=MESH,
+            )
+            out.append((copy, high_side[up] & low[down], low[up] & high_side[down]))
+        return out
+
+    def go(entry):
+        @pl.when(entry[1])
+        def _():
+            entry[0].start()
+
+    def arrive(entry):
+        @pl.when(entry[2])
+        def _():
+            entry[0].wait_recv()
+
+    def start_z(slot, ahead, ref):
         edge_z = 0 if ahead else nz - 1
-        edge_y = 0 if ahead else ny - 1
-        copies = halo_copies(slot, ahead)
-
-        def go(which):
-            copy, sends, _ = copies[which]
-
-            @pl.when(sends)
-            def _():
-                copy.start()
-
         for c in range(2):
-            x_send[slot, c] = ref[1 + c, edge_x]
-        go(0)
+            for x in range(nx):
+                z_send[slot, pl.ds(c * nx + x, 1), :] = ref[c, x, pl.ds(edge_z, 1), :]
+        go(halo_copies(slot, ahead)[2])
+
+    def inner_z(comp, x):
+        here = e_ref[comp, x]
+        return jnp.where(row == nz - 1, 0.0, pltpu.roll(here, nz - 1, 0)) - here
+
+    def start_step(step):
+        down, up, lines = halo_copies(2 * step, True), halo_copies(2 * step + 1, False), edge_copies(step)
+        end = nx - 1
+        for c in range(2):
+            x_send[2 * step, c] = e_ref[1 + c, 0]
+        go(down[0])
+        here = e_ref[0, end]
+        turned = pltpu.roll(here, ny - 1, 1)
+        x_send[2 * step + 1, 0] = h_ref[1, end] - time_step * (inner_z(0, end) + e_ref[2, end])
+        x_send[2 * step + 1, 1] = h_ref[2, end] + time_step * (
+            e_ref[1, end] + (jnp.where(lane == ny - 1, 0.0, turned) - here)
+        )
+        go(up[0])
+        col_send[step, 0] = turned
+        go(lines[2])
+        col_send[step, 1] = pltpu.roll(e_ref[1, 0], (2 * nx - ny) % ny, 1)
+        go(lines[3])
+        row_send[step, 0] = jnp.broadcast_to(e_ref[0, end, pl.ds(0, 1), :], (8, ny))
+        go(lines[0])
         packed = jnp.zeros((nz, ny), F32)
         for c, comp in enumerate((0, 2)):
             for x in range(nx):
                 at = c * nx + x
-                moved = pltpu.roll(ref[comp, x], (at - edge_y) % ny, 1)
-                packed = jnp.where(lane == at, moved, packed)
-        y_send[slot] = packed
-        go(1)
+                packed = jnp.where(lane == at, pltpu.roll(e_ref[comp, x], at, 1), packed)
+        y_send[2 * step] = packed
+        go(down[1])
+        packed = jnp.zeros((nz, ny), F32)
         for c in range(2):
             for x in range(nx):
-                z_send[slot, pl.ds(c * nx + x, 1), :] = ref[c, x, pl.ds(edge_z, 1), :]
-        go(2)
-
-    def finish_halo(slot, ahead):
-        for copy, _, receives in halo_copies(slot, ahead):
-            @pl.when(receives)
-            def _():
-                copy.wait_recv()
+                at = c * nx + x
+                if c == 0:
+                    value = h_ref[0, x] + time_step * (e_ref[2, x] + inner_z(1, x))
+                else:
+                    change = e_ref[1, x + 1] - e_ref[1, x] if x < end else -e_ref[1, x]
+                    value = h_ref[2, x] - time_step * (change + e_ref[0, x])
+                packed = jnp.where(lane == at, pltpu.roll(value, at + 1, 1), packed)
+        y_send[2 * step + 1] = packed
+        go(up[1])
+        line = jnp.zeros((8, ny), F32)
+        for x in range(nx):
+            line = jnp.where(
+                lane[0:8] == x, pltpu.roll(e_ref[1, x, pl.ds(0, 8), :], x + 1, 1), line
+            )
+        row_send[step, 1] = line
+        go(lines[1])
+        start_z(2 * step, True, e_ref)
+
+    def finish_step(step):
+        for entry in halo_copies(2 * step, True):
+            arrive(entry)
+        for entry in halo_copies(2 * step + 1, False)[:2] + edge_copies(step):
+            arrive(entry)
+        slot = 2 * step + 1
+        last_row, last_lane = row == nz - 1, lane == ny - 1
+        line = jnp.broadcast_to(row_recv[step, 0, pl.ds(0, 1), :], (nz, ny))
+        plane = x_recv[slot, 0] + time_step * (e_ref[2, 0] - jnp.where(last_row, line, 0.0))
+        x_recv[slot, 0] = jnp.where(gx > 0, plane, 0.0)
+        plane = x_recv[slot, 1] - time_step * (
+            e_ref[1, 0] - jnp.where(last_lane, col_recv[step, 0], 0.0)
+        )
+        x_recv[slot, 1] = jnp.where(gx > 0, plane, 0.0)
+        own = y_send[2 * step]
+        own = jnp.where(lane < nx, -pltpu.roll(own, ny - nx, 1), pltpu.roll(own, nx, 1))
+        line = jnp.broadcast_to(row_recv[step, 1, pl.ds(0, 1), :], (nz, ny))
+        own = own + jnp.where(last_row & (lane < nx), line, 0.0)
+        own = own - jnp.where(lane == 2 * nx - 1, col_recv[step, 1], 0.0)
+        y_recv[slot] = jnp.where(gy > 0, y_recv[slot] + time_step * own, 0.0)
 
     def curl(ref, slot, ahead, x, packed):
         def dx(comp):
@@ -168,8 +249,8 @@
         lax.fori_loop(0, nx, body, 0)
 
     loads[0].wait()
-    start_halo(0, True, e_ref)
     loads[1].wait()
+    start_step(0)
     loads[2].wait()
     for x in range(nx):
         which = mat[x]
@@ -183,19 +264,17 @@
         drive_ref[x] = time_step * inv_cell / (1.0 + loss)
         g_ref[x] = jnp.zeros((nz, ny), F32)
     loads[3].wait()
-    weighted(0)
+    for c in range(3):
+        weighted(c)
     for step in range(STEPS):
-        finish_halo(2 * step, True)
+        finish_step(step)
         packed = y_recv[2 * step]
         for x in range(nx):
             parts = curl(e_ref, 2 * step, True, x, packed)
             for c in range(3):
                 h_ref[c, x] = h_ref[c, x] - time_step * parts[c]
-        start_halo(2 * step + 1, False, h_ref)
-        if step == 0:
-            weighted(1)
-            weighted(2)
-        finish_halo(2 * step + 1, False)
+        start_z(2 * step + 1, False, h_ref)
+        arrive(halo_copies(2 * step + 1, False)[2])
         packed = y_recv[2 * step + 1]
         for x in range(nx):
             parts = curl(h_ref, 2 * step + 1, False, x, packed)
@@ -203,7 +282,7 @@
             for c in range(3):
                 e_ref[c, x] = decay * e_ref[c, x] + drive * parts[c]
         if step < STEPS - 1:
-            start_halo(2 * step + 2, True, e_ref)
+            start_step(step + 1)
         for x in range(nx):
             g_ref[x] = g_ref[x] + (
                 e_ref[0, x] * q_ref[step, 0, x]
@@ -298,6 +377,11 @@
     lax.fori_loop(1, peers, send_part, 0)
     for slot in range(2 * STEPS):
         for copy, sends, _ in halo_copies(slot, slot % 2 == 0):
+            @pl.when(sends)
+            def _():
+                copy.wait_send()
+    for step in range(STEPS):
+        for copy, sends, _ in edge_copies(step):
             @pl.when(sends)
             def _():
                 copy.wait_send()
@@ -365,11 +449,16 @@
             pltpu.VMEM((slots, 2, nz, ny), F32),
             pltpu.VMEM((slots, 2 * nx, ny), F32),
             pltpu.VMEM((slots, nz, ny), F32),
+            pltpu.VMEM((STEPS, 2, 8, ny), F32),
+            pltpu.VMEM((STEPS, 2, nz, ny), F32),
+            pltpu.VMEM((STEPS, 2, 8, ny), F32),
+            pltpu.VMEM((STEPS, 2, nz, ny), F32),
             pltpu.VMEM((n_gz, tall, ny), F32),
             pltpu.VMEM((peers - 1, tall, ny), F32),
             pltpu.SemaphoreType.DMA((6,)),
             pltpu.SemaphoreType.DMA((slots, 3)),
             pltpu.SemaphoreType.DMA((slots, 3)),
+            pltpu.SemaphoreType.DMA((2, STEPS, 4)),
             pltpu.SemaphoreType.DMA((2,)),
         ],
         compiler_params=pltpu.CompilerParams(

time: 48.9 us -> 42.7 us (0.87)
  Pallas kernels: 40.1 us -> 33.8 us
    pallas_call x1, Pallas kernels: 40.1 us -> 33.8 us  [on_device(): pl.pallas_call(functools.partial(kernel, n_gx, n_gy, n_gz), out_shape=(ja...]
where the time goes in v3:
time: 42.7 us; the launch traced here: 42.4 us
  Pallas kernels  33.8 us (79%)
  local copies, waits for them, and re-layouts  5.83 us (14%)
  other arithmetic  2.1 us (5%)
  between operations  0.64 us (1%)
    pallas_call x1, Pallas kernels, on_device(): pl.pallas_call(functools.partial(kernel, n_gx, n_gy, n_gz), out_shape=(ja...  33.8 us
    unnamed x4, local copies, waits for them, and re-layouts  5.83 us

profile of v3, /device:TPU:0, one launch (start us, length us, event | category | flops | bytes accessed | tf_op | source)
XLA Modules:
  0.0 42.4 jit_solution(15077589761870824713)
XLA Ops:
  0.6 0.7 %neg.4 = f32[16]{0:T(128)S(1)} negate(f32[16]{0:T(128)} %param.18) | non-fusion elementwise | flops 16 | bytes 128 | tf_op jit(solution)/shard_map/neg | solution.py:416
  1.3 0.8 %fusion.1 = (bf16[4,16]{1,0:T(4,128)(2,1)S(1)}, bf16[4,16]{1,0:T(4,128)(2,1)S(1)}) fusion(f32[16]{0:T(128)} %param.17, f32[4]{0:T(128)S(1)} %convert_multiply_fusion, f32[16]{0:T(128)} %param.18, f32[16]{0:T(128)S(1)} %neg.4), kind=kLoop, calls=%fused_computation.3 | loop fusion | flops 320 | bytes 464 | tf_op jit(solution)/shard_map/convert
  2.1 0.7 %maximum_convert_fusion.phase = f32[4,32]{1,0:T(4,128)} fusion(bf16[4,16]{1,0:T(4,128)(2,1)S(1)} %get-tuple-element.4, bf16[4,16]{1,0:T(4,128)(2,1)S(1)} %get-tuple-element.3), kind=kLoop, calls=%fused_computation.6 | loop fusion | flops 512 | bytes 768 | tf_op jit(solution)/shard_map/convert_element_type | solution.py:417
  2.7 1.3 %copy.14.owner_map = s32[4,2]{1,0:T(4,128)} copy(s32[4,2]{0,1:T(2,128)} %param.21) | data formatting | bytes 64 | tf_op args[10]
  4.1 33.8 %shard_map.130 = (f32[3,8,16,128]{3,2,1,0:T(8,128)}, f32[3,8,16,128]{3,2,1,0:T(8,128)}, f32[1,512]{1,0:T(1,128)}) custom-call(f32[4,32]{1,0:T(4,128)} %maximum_convert_fusion.phase, f32[4]{0:T(128)} %inv_eps.1, f32[4]{0:T(128)} %cond.1, s32[4,2]{1,0:T(4,128)} %copy.14.owner_map, f32[3,8,16,128]{3,2,1,0:T(8,128)} %e_hbm.1, f32[3,8,16,128]{3,2,1,0:T(8,128)} %h_hbm.1, ...), custom_call_target="tpu_custom_call" | custom-call | tf_op jit(solution)/shard_map/pallas_call | solution.py:425
  37.9 1.6 %copy.18 = f32[3,8,16,128]{3,2,1,0:T(8,128)} copy(f32[3,8,16,128]{3,2,1,0:T(8,128)} %get-tuple-element.8) | data formatting | bytes 393216
  39.5 1.6 %copy.19 = f32[3,8,16,128]{3,2,1,0:T(8,128)} copy(f32[3,8,16,128]{3,2,1,0:T(8,128)} %get-tuple-element.9) | data formatting | bytes 393216
  41.1 1.3 %copy.20 = f32[1,512]{1,0:T(1,128)} copy(f32[1,512]{1,0:T(1,128)} %get-tuple-element.10) | data formatting | bytes 4096
  (1 shorter events, 0.0 us)

commit v4 on v3

--- a/solution.py
+++ b/solution.py
@@ -18,7 +18,7 @@
 
 def kernel(
     n_gx, n_gy, n_gz,
-    phase, inv_eps, cond, owner_map,
+    phase_re, phase_im, inv_eps, cond, owner_map,
     e_hbm, h_hbm, dft_hbm, mat_hbm, sten_hbm, w_hbm,
     e_ref, h_ref, grad_ref,
     dft, mat, sten, wgt, q_ref, decay_ref, drive_ref, g_ref,
@@ -33,6 +33,7 @@
     part = lax.axis_index("parts")
     gx, gy, gz = lax.axis_index("gx"), lax.axis_index("gy"), lax.axis_index("gz")
     peers = n_gx * n_gy * n_gz
+    freqs = freqs2 // 2
     me = (gx * n_gy + gy) * n_gz + gz
 
     def place(rank):
@@ -241,7 +242,8 @@
             for f in range(freqs2):
                 value = dft[f, c, x].astype(F32)
                 for t in range(STEPS):
-                    sums[t] = sums[t] + phase[t, f] * value
+                    factor = phase_re[t, f] if f < freqs else phase_im[t, f - freqs]
+                    sums[t] = sums[t] + factor * value
             for t in range(STEPS):
                 q_ref[t, c, x] = sums[t]
             return carry
@@ -389,11 +391,11 @@
     pltpu.make_async_copy(p_recv, p_recv, p_sems.at[0]).wait()
 
     my_owner = gx * n_gy + gy
-    mine = jnp.where(owner_map[gx, gy] == my_owner, p_send[gz], 0.0)
+    mine = jnp.where(owner_map[gy, gx] == my_owner, p_send[gz], 0.0)
 
     def add_part(d, total):
         brick = lax.rem(me - d + peers, peers) // n_gz
-        owner = owner_map[brick // n_gy, brick % n_gy]
+        owner = owner_map[brick % n_gy, brick // n_gy]
         return total + jnp.where(owner == my_owner, p_recv[d - 1], 0.0)
 
     mine = lax.fori_loop(1, peers, add_part, mine)
@@ -412,9 +414,8 @@
     peers = n_gx * n_gy * n_gz
     times = (jnp.arange(STEPS) + 1).astype(F32) * time_step
     angles = times[:, None] * omega[None, :]
-    phase = jnp.concatenate(
-        [freq_weight[None, :] * jnp.cos(angles), -freq_weight[None, :] * jnp.sin(angles)], axis=1
-    ).astype(BF16).astype(F32)
+    phase_re = lax.reduce_precision(freq_weight[None, :] * jnp.cos(angles), 8, 7)
+    phase_im = lax.reduce_precision(-(freq_weight[None, :] * jnp.sin(angles)), 8, 7)
     dft = forward_dft.reshape(2 * freqs, 3, nx, nz, ny)
     smem = pl.BlockSpec(memory_space=pltpu.SMEM)
     hbm = pl.BlockSpec(memory_space=pl.ANY)
@@ -429,7 +430,7 @@
             jax.ShapeDtypeStruct(h_adjoint.shape, F32),
             jax.ShapeDtypeStruct((1, PS // n_gz), F32),
         ),
-        in_specs=[smem] * 4 + [hbm] * 6,
+        in_specs=[smem] * 5 + [hbm] * 6,
         out_specs=(vmem, vmem, vmem),
         scratch_shapes=[
             pltpu.VMEM(dft.shape, BF16),
@@ -464,7 +465,7 @@
         compiler_params=pltpu.CompilerParams(
             collective_id=0, has_side_effects=True, vmem_limit_bytes=60 * 1024 * 1024
         ),
-    )(phase, inv_permittivity, conductivity, owner_map,
+    )(phase_re, phase_im, inv_permittivity, conductivity, owner_map.T,
       e_adjoint, h_adjoint, dft, material, stencil, stencil_weight)
 
 

time: 42.7 us -> 40.6 us (0.951)
  local copies, waits for them, and re-layouts: 5.83 us -> 4.49 us
  other arithmetic: 2.1 us -> 1.38 us
    reduce_precision x0 -> x1, other arithmetic: none -> 1.37 us  [on_device(): lax.reduce_precision(-(freq_weight[None, :] * jnp.sin(angles)), 8, 7)]
    unnamed x4 -> x3, local copies, waits for them, and re-layouts: 5.83 us -> 4.49 us
    another operation x1 -> x0, other arithmetic: 0.78 us -> none
    neg x1 -> x0, other arithmetic: 0.66 us -> none  [on_device(): -freq_weight[None, :] * jnp.sin(angles)]
    convert_element_type x1 -> x0, other arithmetic: 0.66 us -> none  [on_device(): phase = jnp.concatenate([freq_weight[None, :] * jnp.cos(angles), -freq_we...]
where the time goes in v4:
time: 40.6 us; the launch traced here: 40.4 us
  Pallas kernels  33.9 us (83%)
  local copies, waits for them, and re-layouts  4.49 us (11%)
  other arithmetic  1.38 us (3%)
  between operations  0.64 us (2%)
    pallas_call x1, Pallas kernels, on_device(): pl.pallas_call(functools.partial(kernel, n_gx, n_gy, n_gz), out_shape=(ja...  33.9 us
    unnamed x3, local copies, waits for them, and re-layouts  4.49 us
    reduce_precision x1, other arithmetic, on_device(): lax.reduce_precision(-(freq_weight[None, :] * jnp.sin(angles)), 8, 7)  1.37 us

profile of v4, /device:TPU:0, one launch (start us, length us, event | category | flops | bytes accessed | tf_op | source)
XLA Modules:
  0.0 40.4 jit_solution(12137031637407459357)
XLA Ops:
  0.6 1.4 %fusion.4 = (f32[4,16]{1,0:T(4,128)}, f32[4,16]{1,0:T(4,128)}) fusion(f32[16]{0:T(128)} %param.17, f32[4]{0:T(128)S(1)} %convert_multiply_fusion, f32[16]{0:T(128)} %param.18), kind=kLoop, calls=%fused_computation.6 | loop fusion | flops 384 | bytes 656 | tf_op jit(solution)/shard_map/reduce_precision | solution.py:418
  2.0 33.9 %shard_map.130 = (f32[3,8,16,128]{3,2,1,0:T(8,128)}, f32[3,8,16,128]{3,2,1,0:T(8,128)}, f32[1,512]{1,0:T(1,128)}) custom-call(f32[4,16]{1,0:T(4,128)} %get-tuple-element.4.phase_re, f32[4,16]{1,0:T(4,128)} %get-tuple-element.3.phase_im, f32[4]{0:T(128)} %inv_eps.1, f32[4]{0:T(128)} %cond.1, s32[2,4]{1,0:T(2,128)} %bitcast.3, f32[3,8,16,128]{3,2,1,0:T(8,128)} %e_hbm.1, ...), custom_call_target="tpu_custom_call" | custom-call | tf_op jit(solution)/shard_map/pallas_call | solution.py:426
  35.9 1.6 %copy.17 = f32[3,8,16,128]{3,2,1,0:T(8,128)} copy(f32[3,8,16,128]{3,2,1,0:T(8,128)} %get-tuple-element.8) | data formatting | bytes 393216
  37.5 1.6 %copy.18 = f32[3,8,16,128]{3,2,1,0:T(8,128)} copy(f32[3,8,16,128]{3,2,1,0:T(8,128)} %get-tuple-element.9) | data formatting | bytes 393216
  39.1 1.3 %copy.19 = f32[1,512]{1,0:T(1,128)} copy(f32[1,512]{1,0:T(1,128)} %get-tuple-element.10) | data formatting | bytes 4096
  (1 shorter events, 0.0 us)
